TPU v7x, 32 devices: a whole 2x2x4 slice. The times are simulated.
32 devices in a mesh: grp: 4 (over x, core), seq: 8 (over z, y).
Axes of the slice: x: 2, y: 2, z: 4, core: 2. Of those that a mesh axis runs over, the one named last changes fastest.
Arguments:
- queries: bfloat16 [4096, 3072], P(('grp', 'seq')), may hold values from -6 to 6, as said below
- key_states: bfloat16 [4096, 3072], P(('grp', 'seq')), may hold values from -6 to 6
- value_states: bfloat16 [4096, 3072], P(('grp', 'seq')), may hold values from -16 to 16
- key_keep: int32 [4096], P(('grp', 'seq')), may hold values 0 or 1
- summary_pos: int32 [4], replicated, may hold values from 0 to 7
Outputs:
- attended: bfloat16 [4096, 3072], P(('grp', 'seq'))
Inputs may be any that keep to these rules, and one draw needn't show every extreme that they name: queries and key_states entries lie within -6 to 6.
All inputs are finite; a program needn't handle non-finite values. No bound on the sum of `key_keep` on one device may be relied on, other than what follows from the above.
Results may differ from a plain program's by a relative error of at most 0.008.
Values may be sent and summed in bfloat16 or wider, within the bound.
A program may use at most 64 MiB of HBM per device.

v0:
```python
import math

import jax
import jax.numpy as jnp
from jax import lax
from jax.sharding import PartitionSpec as P

HEADS = 24
HEAD_DIM = 128
FIXED_HEADS = 4
STRIDED_HEADS = 4
LOCAL_HEADS = 16
BLOCK = 128
LOOKBACK = 2


NEG = -1e30


def passed_along(block, axis, distance):
    devices = range(lax.axis_size(axis))
    route = [(i - distance, i) for i in devices if i - distance in devices]
    return lax.ppermute(block, axis, route)


def spread(value, axis, source):
    kept = jnp.where(lax.axis_index(axis) == source, value, 0).astype(value.dtype)
    return lax.psum(kept, axis)


def partial_softmax(query_heads, key_rows, value_rows, allowed):
    scores = jnp.einsum(
        "qhd,khd->hqk", query_heads, key_rows, preferred_element_type=jnp.float32
    ) / math.sqrt(HEAD_DIM)
    scores = jnp.where(allowed[None], scores, NEG)
    row_max = jnp.max(scores, axis=2)
    weights = jnp.where(allowed[None], jnp.exp(scores - row_max[:, :, None]), 0.0)
    row_sum = jnp.sum(weights, axis=2)
    weighted = jnp.einsum(
        "hqk,khd->hqd", weights.astype(jnp.bfloat16), value_rows, preferred_element_type=jnp.float32
    )
    return (row_max, row_sum, weighted)


def merge_state(left_part, right_part):
    row_max = jnp.maximum(left_part[0], right_part[0])
    left_scale = jnp.exp(left_part[0] - row_max)
    right_scale = jnp.exp(right_part[0] - row_max)
    row_sum = left_part[1] * left_scale + right_part[1] * right_scale
    weighted = left_part[2] * left_scale[:, :, None] + right_part[2] * right_scale[:, :, None]
    return (row_max, row_sum, weighted)


def blank_state(count):
    return (
        jnp.full((count, BLOCK), NEG, jnp.float32),
        jnp.zeros((count, BLOCK), jnp.float32),
        jnp.zeros((count, BLOCK, HEAD_DIM), jnp.float32),
    )


def head_range(state, head_lo, head_hi):
    return tuple((member[head_lo:head_hi] for member in state))


def on_device(queries, key_states, value_states, key_keep, summary_pos):
    stride = lax.axis_size("seq")
    groups = lax.axis_size("grp")
    column = lax.axis_index("seq")
    window = lax.axis_index("grp")
    block_id = window * stride + column
    lane_ids = jnp.arange(BLOCK, dtype=jnp.int32)
    group_ids = jnp.arange(groups, dtype=jnp.int32)
    query_heads = queries.reshape(BLOCK, HEADS, HEAD_DIM)
    keep_flag = key_keep.astype(jnp.bfloat16)
    own_block = (key_states, value_states, keep_flag)

    def all_heads(block_rows, allowed):
        return partial_softmax(
            query_heads,
            block_rows[0].reshape(BLOCK, HEADS, HEAD_DIM),
            block_rows[1].reshape(BLOCK, HEADS, HEAD_DIM),
            allowed,
        )

    diagonal = lane_ids[:, None] == lane_ids[None, :]
    causal = (lane_ids[None, :] <= lane_ids[:, None]) & ((key_keep[None, :] == 1) | diagonal)
    near_state = all_heads(own_block, causal)
    prior_one = passed_along((own_block[0], own_block[1], own_block[2]), ("grp", "seq"), 1)
    prior_two = passed_along((own_block[0], own_block[1], own_block[2]), ("grp", "seq"), 2)
    for earlier in (prior_one, prior_two):
        allowed = jnp.broadcast_to((earlier[2] > 0)[None, :], (BLOCK, BLOCK))
        near_state = merge_state(near_state, all_heads(earlier, allowed))
    fixed_lo = LOCAL_HEADS * HEAD_DIM
    fixed_hi = (LOCAL_HEADS + FIXED_HEADS) * HEAD_DIM
    root_dev = summary_pos[window]
    summary_own = (key_states[:, fixed_lo:fixed_hi], value_states[:, fixed_lo:fixed_hi], keep_flag)
    summary_here = (
        spread(summary_own[0], "seq", root_dev),
        spread(summary_own[1], "seq", root_dev),
        spread(summary_own[2], "seq", root_dev),
    )
    fixed_queries = query_heads[:, LOCAL_HEADS : LOCAL_HEADS + FIXED_HEADS]
    shard_rows = (
        lax.all_gather(summary_here[0], "grp", axis=0, tiled=True),
        lax.all_gather(summary_here[1], "grp", axis=0, tiled=True),
        lax.all_gather(summary_here[2], "grp", axis=0, tiled=True),
    )
    row_count = shard_rows[0].shape[0]
    row_window = jnp.arange(row_count, dtype=jnp.int32) // BLOCK
    hit_mask = row_window[:, None] == group_ids[None, :]
    row_summary = jnp.sum(jnp.where(hit_mask, summary_pos[None, :], 0), axis=1)
    usable = (row_window * stride + row_summary < block_id - LOOKBACK) & (shard_rows[2] > 0)
    allowed = jnp.broadcast_to(usable[None, :], (BLOCK, row_count))
    term = partial_softmax(
        fixed_queries,
        shard_rows[0].reshape(row_count, FIXED_HEADS, HEAD_DIM),
        shard_rows[1].reshape(row_count, FIXED_HEADS, HEAD_DIM),
        allowed,
    )
    fixed_state = merge_state(blank_state(FIXED_HEADS), term)
    column_own = (key_states[:, fixed_hi:], value_states[:, fixed_hi:], keep_flag)
    strided_queries = query_heads[:, LOCAL_HEADS + FIXED_HEADS :]
    shard_rows = (
        lax.all_gather(column_own[0], "grp", axis=0, tiled=True),
        lax.all_gather(column_own[1], "grp", axis=0, tiled=True),
        lax.all_gather(column_own[2], "grp", axis=0, tiled=True),
    )
    row_count = shard_rows[0].shape[0]
    row_window = jnp.arange(row_count, dtype=jnp.int32) // BLOCK
    usable = (row_window < window) & (shard_rows[2] > 0)
    allowed = jnp.broadcast_to(usable[None, :], (BLOCK, row_count))
    term = partial_softmax(
        strided_queries,
        shard_rows[0].reshape(row_count, STRIDED_HEADS, HEAD_DIM),
        shard_rows[1].reshape(row_count, STRIDED_HEADS, HEAD_DIM),
        allowed,
    )
    strided_state = merge_state(blank_state(STRIDED_HEADS), term)
    local_total = head_range(near_state, 0, LOCAL_HEADS)
    fixed_total = merge_state(
        head_range(near_state, LOCAL_HEADS, LOCAL_HEADS + FIXED_HEADS), fixed_state
    )
    strided_total = merge_state(
        head_range(near_state, LOCAL_HEADS + FIXED_HEADS, HEADS), strided_state
    )
    row_sum = jnp.concatenate([local_total[1], fixed_total[1], strided_total[1]], axis=0)
    weighted = jnp.concatenate([local_total[2], fixed_total[2], strided_total[2]], axis=0)
    result = weighted / row_sum[:, :, None]
    return jnp.transpose(result, (1, 0, 2)).reshape(BLOCK, HEADS * HEAD_DIM).astype(jnp.bfloat16)


def solution(mesh):
    return jax.shard_map(
        on_device,
        mesh=mesh,
        in_specs=(
            P(("grp", "seq"), None),
            P(("grp", "seq"), None),
            P(("grp", "seq"), None),
            P(("grp", "seq")),
            P(),
        ),
        out_specs=P(("grp", "seq"), None),
        check_vma=False,
    )
```

profile of v0, /device:TPU:3, one launch (start us, length us, event | category | flops | bytes accessed | tf_op | source)
XLA Modules:
  0.0 174.3 jit_solution(14604299937531128261)
XLA Ops:
  6.5 0.7 convert_bitcast_fusion
  7.2 3.3 %collective-permute-start = (bf16[128]{0:T(256)(128)(2,1)S(1)}, bf16[128]{0:T(256)(128)(2,1)S(1)}, u32[]{:S(2)}, u32[]{:S(2)}) collective-permute-start(bf16[128]{0:T(256)(128)(2,1)S(1)} %get-tuple-element.37), channel_id=1, source_target_pairs={{0,1},{1,2},{2,3},{3,4},{4,5},{5,6},{6,7},{7,8},{8,9},{9,10},{10,1... | collective-permute-start | bytes 776 | tf_op jit(solution)/shard_map/ppermute | solution.py:23
  10.5 3.2 %collective-permute-start.3 = (bf16[128]{0:T(256)(128)(2,1)S(1)}, bf16[128]{0:T(256)(128)(2,1)S(1)}, u32[]{:S(2)}, u32[]{:S(2)}) collective-permute-start(bf16[128]{0:T(256)(128)(2,1)S(1)} %get-tuple-element.37), channel_id=1, source_target_pairs={{0,2},{1,3},{2,4},{3,5},{4,6},{5,7},{6,8},{7,9},{8,10},{9,11},{10,... | collective-permute-start | bytes 776 | tf_op jit(solution)/shard_map/ppermute | solution.py:23
  13.7 2.3 %copy.78 = bf16[128,3072]{0,1:T(8,128)(2,1)} copy(bf16[128,3072]{1,0:T(8,128)(2,1)} %param.6) | data formatting | bytes 1572864 | tf_op args[1]
  16.0 3.3 %collective-permute-start.1 = (bf16[128,3072]{0,1:T(8,128)(2,1)}, bf16[128,3072]{0,1:T(8,128)(2,1)}, u32[]{:S(2)}, u32[]{:S(2)}) collective-permute-start(bf16[128,3072]{0,1:T(8,128)(2,1)} %copy.78), channel_id=1, source_target_pairs={{0,1},{1,2},{2,3},{3,4},{4,5},{5,6},{6,7},{7,8},{8,9},{9,10},{10,1... | collective-permute-start | bytes 2359304 | tf_op jit(solution)/shard_map/ppermute | solution.py:23
  19.3 3.2 %collective-permute-start.4 = (bf16[128,3072]{0,1:T(8,128)(2,1)}, bf16[128,3072]{0,1:T(8,128)(2,1)}, u32[]{:S(2)}, u32[]{:S(2)}) collective-permute-start(bf16[128,3072]{0,1:T(8,128)(2,1)} %copy.78), channel_id=1, source_target_pairs={{0,2},{1,3},{2,4},{3,5},{4,6},{5,7},{6,8},{7,9},{8,10},{9,11},{10,... | collective-permute-start | bytes 2359304 | tf_op jit(solution)/shard_map/ppermute | solution.py:23
  22.5 3.2 %collective-permute-start.2 = (bf16[128,3072]{1,0:T(8,128)(2,1)}, bf16[128,3072]{1,0:T(8,128)(2,1)}, u32[]{:S(2)}, u32[]{:S(2)}) collective-permute-start(bf16[128,3072]{1,0:T(8,128)(2,1)} %param.7), channel_id=1, source_target_pairs={{0,1},{1,2},{2,3},{3,4},{4,5},{5,6},{6,7},{7,8},{8,9},{9,10},{10,1... | collective-permute-start | bytes 2359304 | tf_op jit(solution)/shard_map/ppermute | solution.py:23
  25.6 1.5 copy.113
  27.2 0.7 dynamic_slice.3
  28.5 1.6 slice_select_fusion.1
  30.2 0.7 slice_select_fusion
  30.9 0.9 slice.52
  31.8 47.3 %psum.21 = bf16[128]{0:T(256)(128)(2,1)S(1)} all-reduce(bf16[128]{0:T(256)(128)(2,1)S(1)} %broadcast_select_fusion), channel_id=1, replica_groups=mesh['grp'=4,'seq'=8] {'seq'}, use_global_device_ids=true, to_apply=%region_4.5 | all-reduce | flops 128 | bytes 512 | tf_op jit(solution)/shard_map/psum | solution.py:28
  79.1 10.3 %all-gather = bf16[4,1,128]{2,1,0:T(2,128)(2,1)S(1)} all-gather(bf16[1,1,128]{2,1,0:T(2,128)(2,1)S(1)} %bitcast.58), channel_id=1, replica_groups=mesh['grp'=4,'seq'=8] {'grp'}, dimensions={0}, use_global_device_ids=true | all-gather | bytes 1280 | tf_op jit(solution)/shard_map/all_gather | solution.py:107
  90.0 8.2 %all_gather.22 = bf16[512,512]{0,1:T(8,128)(2,1)} all-gather(bf16[128,512]{0,1:T(8,128)(2,1)S(1)} %get-tuple-element.20), channel_id=1, replica_groups=mesh['grp'=4,'seq'=8] {'grp'}, dimensions={0}, use_global_device_ids=true | all-gather | bytes 655360 | tf_op jit(solution)/shard_map/all_gather | solution.py:125
  98.2 5.0 %all-gather.1 = bf16[4,1,128]{2,1,0:T(2,128)(2,1)S(1)} all-gather(bf16[1,1,128]{2,1,0:T(2,128)(2,1)S(1)} %get-tuple-element.36), channel_id=1, replica_groups=mesh['grp'=4,'seq'=8] {'grp'}, dimensions={0}, use_global_device_ids=true | all-gather | bytes 1280 | tf_op jit(solution)/shard_map/all_gather | solution.py:127
  104.0 1.5 fusion.21
  106.0 7.3 %all_gather.23 = bf16[512,512]{1,0:T(8,128)(2,1)S(1)} all-gather(bf16[128,512]{1,0:T(8,128)(2,1)S(1)} %slice.52), channel_id=1, replica_groups=mesh['grp'=4,'seq'=8] {'grp'}, dimensions={0}, use_global_device_ids=true | all-gather | bytes 655360 | tf_op jit(solution)/shard_map/all_gather | solution.py:126
  113.3 1.0 copy.97
  114.3 1.9 %collective-permute-start.5 = (bf16[128,3072]{1,0:T(8,128)(2,1)}, bf16[128,3072]{1,0:T(8,128)(2,1)}, u32[]{:S(2)}, u32[]{:S(2)}) collective-permute-start(bf16[128,3072]{1,0:T(8,128)(2,1)} %param.7), channel_id=1, source_target_pairs={{0,2},{1,3},{2,4},{3,5},{4,6},{5,7},{6,8},{7,9},{8,10},{9,11},{10,... | collective-permute-start | bytes 2359304 | tf_op jit(solution)/shard_map/ppermute | solution.py:23
  116.3 13.7 %all-reduce.3.cloned.1.call-done = (bf16[128,512]{0,1:T(8,128)(2,1)}, bf16[128,512]{0,1:T(8,128)(2,1)}) async-done(((bf16[128,512]{0,1:T(8,128)(2,1)}, bf16[128,512]{0,1:T(8,128)(2,1)}), (bf16[128,512]{0,1:T(8,128)(2,1)}, bf16[128,512]{0,1:T(8,128)(2,1)})) %all-reduce.3.cloned.1.call-update) | async-done | bytes 262160 | tf_op jit(solution)/shard_map/psum | solution.py:28
  130.0 10.7 %all_gather.19 = bf16[512,512]{0,1:T(8,128)(2,1)S(1)} all-gather(bf16[128,512]{0,1:T(8,128)(2,1)} %get-tuple-element.5), channel_id=1, replica_groups=mesh['grp'=4,'seq'=8] {'grp'}, dimensions={0}, use_global_device_ids=true | all-gather | bytes 655360 | tf_op jit(solution)/shard_map/all_gather | solution.py:105
  140.6 8.0 %all_gather.20 = bf16[512,512]{0,1:T(8,128)(2,1)} all-gather(bf16[128,512]{0,1:T(8,128)(2,1)} %get-tuple-element.6), channel_id=1, replica_groups=mesh['grp'=4,'seq'=8] {'grp'}, dimensions={0}, use_global_device_ids=true | all-gather | bytes 655360 | tf_op jit(solution)/shard_map/all_gather | solution.py:106
  149.4 0.6 copy-done.2
  150.0 1.6 fusion.76
  151.6 1.8 %fusion.78 = (f32[24,128]{1,0:T(8,128)S(1)}, f32[24,128,128]{1,2,0:T(8,128)S(1)}) fusion(bf16[128,24,128]{0,2,1:T(8,128)(2,1)} %bitcast.49, bf16[128,24,128]{0,2,1:T(8,128)(2,1)} %bitcast.4, pred[128]{0:T(512)(128)(4,1)S(1)} %broadcast_compare_fusion), kind=kOutput, calls=%fused_computation.116 | convolution fusion | flops 101839872 | bytes 3158144 | tf_op jit(solution)/shard_map/qhd,khd->hqk/dot_general | solution.py:32
  154.1 2.3 %copy.81 = bf16[128,3072]{0,1:T(8,128)(2,1)} copy(bf16[128,3072]{1,0:T(8,128)(2,1)} %collective-permute-done.2) | data formatting | bytes 1572864 | tf_op jit(solution)/shard_map/ppermute | solution.py:23
  156.4 2.7 %fusion.19 = f32[24,128,128]{1,2,0:T(8,128)} fusion(bf16[128,24,128]{0,2,1:T(8,128)(2,1)} %bitcast.51, f32[24,128,128]{1,2,0:T(8,128)S(1)} %get-tuple-element.39, f32[24,128]{1,0:T(8,128)S(1)} %get-tuple-element.38, pred[128]{0:T(512)(128)(4,1)S(1)} %broadcast_compare_fusion.1), kind=kOutput, calls=%fused_computation.32 | convolution fusion | flops 101842944 | bytes 3944576 | tf_op jit(solution)/shard_map/hqk,khd->hqd/dot_general | solution.py:39
  159.1 2.4 %copy.86 = bf16[128,3072]{0,1:T(8,128)(2,1)} copy(bf16[128,3072]{1,0:T(8,128)(2,1)} %collective-permute-done.5) | data formatting | bytes 1572864 | tf_op jit(solution)/shard_map/ppermute | solution.py:23
  161.5 2.3 %multiply_add_fusion = f32[24,128,128]{1,2,0:T(8,128)S(1)} fusion(f32[24,128,128]{1,2,0:T(8,128)S(1)} %copy-done.1, f32[24,128,128]{1,2,0:T(8,128)} %fusion.21, bf16[128,24,128]{0,2,1:T(8,128)(2,1)} %bitcast.53, f32[24,128,128]{1,2,0:T(8,128)S(1)} %get-tuple-element.43, f32[24,128]{1,0:T(8,128)S(1)} %get-tuple-element.17, ...), kind=kOutput, calls=%fused_computation.2 | convolution fusion | flops 104202240 | bytes 7139456 | tf_op jit(solution)/shard_map/hqk,khd->hqd/dot_general | solution.py:39
  164.0 1.1 copy-done.3
  166.3 1.2 copy.99
  (59 shorter events, 4.6 us)
Async XLA Ops:
  6.5 123.4 %all-reduce.3.cloned.1.call-start = ((), (), s32[]{:S(2)}) async-start(), calls=%async_computation | async-start | bytes 524288 | tf_op jit(solution)/shard_map/psum | solution.py:28
  7.2 20.0 %copy-start.11 = (s32[4]{0:T(128)S(1)}, s32[4]{0:T(128)}, u32[]{:S(2)}) copy-start(s32[4]{0:T(128)} %param.9) | copy-start | bytes 52
  7.2 107.1 %collective-permute-start = (bf16[128]{0:T(256)(128)(2,1)S(1)}, bf16[128]{0:T(256)(128)(2,1)S(1)}, u32[]{:S(2)}, u32[]{:S(2)}) collective-permute-start(bf16[128]{0:T(256)(128)(2,1)S(1)} %get-tuple-element.37), channel_id=1, source_target_pairs={{0,1},{1,2},{2,3},{3,4},{4,5},{5,6},{6,7},{7,8},{8,9},{9,10},{10,1... | collective-permute-start | bytes 776 | tf_op jit(solution)/shard_map/ppermute | solution.py:23
  10.5 105.8 %collective-permute-start.3 = (bf16[128]{0:T(256)(128)(2,1)S(1)}, bf16[128]{0:T(256)(128)(2,1)S(1)}, u32[]{:S(2)}, u32[]{:S(2)}) collective-permute-start(bf16[128]{0:T(256)(128)(2,1)S(1)} %get-tuple-element.37), channel_id=1, source_target_pairs={{0,2},{1,3},{2,4},{3,5},{4,6},{5,7},{6,8},{7,9},{8,10},{9,11},{10,... | collective-permute-start | bytes 776 | tf_op jit(solution)/shard_map/ppermute | solution.py:23
  16.0 14.9 %copy-start.12 = (s32[128]{0:T(128)S(1)}, s32[128]{0:T(128)}, u32[]{:S(2)}) copy-start(s32[128]{0:T(128)} %param.8) | copy-start | bytes 1540
  16.0 73.6 %copy-start.6 = (bf16[128,3072]{1,0:T(8,128)(2,1)S(1)}, bf16[128,3072]{1,0:T(8,128)(2,1)}, u32[]{:S(2)}) copy-start(bf16[128,3072]{1,0:T(8,128)(2,1)} %param.5) | copy-start | bytes 2359300
  16.0 133.4 %collective-permute-start.1 = (bf16[128,3072]{0,1:T(8,128)(2,1)}, bf16[128,3072]{0,1:T(8,128)(2,1)}, u32[]{:S(2)}, u32[]{:S(2)}) collective-permute-start(bf16[128,3072]{0,1:T(8,128)(2,1)} %copy.78), channel_id=1, source_target_pairs={{0,1},{1,2},{2,3},{3,4},{4,5},{5,6},{6,7},{7,8},{8,9},{9,10},{10,1... | collective-permute-start | bytes 2359304 | tf_op jit(solution)/shard_map/ppermute | solution.py:23
  19.3 132.3 %collective-permute-start.4 = (bf16[128,3072]{0,1:T(8,128)(2,1)}, bf16[128,3072]{0,1:T(8,128)(2,1)}, u32[]{:S(2)}, u32[]{:S(2)}) collective-permute-start(bf16[128,3072]{0,1:T(8,128)(2,1)} %copy.78), channel_id=1, source_target_pairs={{0,2},{1,3},{2,4},{3,5},{4,6},{5,7},{6,8},{7,9},{8,10},{9,11},{10,... | collective-permute-start | bytes 2359304 | tf_op jit(solution)/shard_map/ppermute | solution.py:23
  22.5 131.6 %collective-permute-start.2 = (bf16[128,3072]{1,0:T(8,128)(2,1)}, bf16[128,3072]{1,0:T(8,128)(2,1)}, u32[]{:S(2)}, u32[]{:S(2)}) collective-permute-start(bf16[128,3072]{1,0:T(8,128)(2,1)} %param.7), channel_id=1, source_target_pairs={{0,1},{1,2},{2,3},{3,4},{4,5},{5,6},{6,7},{7,8},{8,9},{9,10},{10,1... | collective-permute-start | bytes 2359304 | tf_op jit(solution)/shard_map/ppermute | solution.py:23
  30.2 73.1 %copy-start.7 = (bf16[128,3072]{1,0:T(8,128)(2,1)S(1)}, bf16[128,3072]{1,0:T(8,128)(2,1)}, u32[]{:S(2)}) copy-start(bf16[128,3072]{1,0:T(8,128)(2,1)} %param.6) | copy-start | bytes 2359300
  90.0 60.0 %copy-start = (bf16[128,3072]{0,1:T(8,128)(2,1)}, bf16[128,3072]{0,1:T(8,128)(2,1)S(1)}, u32[]{:S(2)}) copy-start(bf16[128,3072]{0,1:T(8,128)(2,1)S(1)} %copy.73) | copy-start | bytes 2359300
  104.0 1.6 copy-start.9
  106.0 43.0 %copy-start.4 = (f32[4,128,512]{1,2,0:T(8,128)}, f32[4,128,512]{1,2,0:T(8,128)S(1)}, u32[]{:S(2)}) copy-start(f32[4,128,512]{1,2,0:T(8,128)S(1)} %get-tuple-element.47) | copy-start | bytes 3145732
  114.3 44.8 %collective-permute-start.5 = (bf16[128,3072]{1,0:T(8,128)(2,1)}, bf16[128,3072]{1,0:T(8,128)(2,1)}, u32[]{:S(2)}, u32[]{:S(2)}) collective-permute-start(bf16[128,3072]{1,0:T(8,128)(2,1)} %param.7), channel_id=1, source_target_pairs={{0,2},{1,3},{2,4},{3,5},{4,6},{5,7},{6,8},{7,9},{8,10},{9,11},{10,... | collective-permute-start | bytes 2359304 | tf_op jit(solution)/shard_map/ppermute | solution.py:23
  149.0 1.0 copy-start.2
  159.1 2.4 %copy-start.1 = (f32[24,128,128]{1,2,0:T(8,128)S(1)}, f32[24,128,128]{1,2,0:T(8,128)}, u32[]{:S(2)}) copy-start(f32[24,128,128]{1,2,0:T(8,128)} %fusion.19) | copy-start | bytes 4718596
  163.8 1.2 copy-start.3
  163.8 1.3 copy-start.8
  163.9 1.7 copy-start.5
  163.9 1.7 copy-start.10
Sparse Core Ops, SparseCore 0:
  31.0 98.9 all-reduce.2
where the time goes:
time: 177 us; the launch traced here: 174 us
  blocking collectives  96.8 us (55%)
  starting transfers between devices  18 us (10%)
  local copies, waits for them, and re-layouts  14.6 us (8%)
  between operations  14.4 us (8%)
  waiting for transfers between devices  13.7 us (8%)
  matrix products  12 us (7%)
  other arithmetic  4.81 us (3%)
    psum x1, blocking collectives, spread(): return lax.psum(kept, axis)  47.3 us
    ppermute x6, starting transfers between devices, passed_along(): return lax.ppermute(block, axis, route)  18 us
    psum x1, waiting for transfers between devices, spread(): return lax.psum(kept, axis)  13.7 us
    all_gather x1, blocking collectives, on_device(): lax.all_gather(summary_here[0], 'grp', axis=0, tiled=True)  10.7 us
    all_gather x1, blocking collectives, on_device(): lax.all_gather(summary_here[2], 'grp', axis=0, tiled=True)  10.3 us
    all_gather x1, blocking collectives, on_device(): lax.all_gather(column_own[0], 'grp', axis=0, tiled=True)  8.22 us
    all_gather x1, blocking collectives, on_device(): lax.all_gather(summary_here[1], 'grp', axis=0, tiled=True)  7.95 us
    dot_general x5, matrix products, partial_softmax(): jnp.einsum('hqk,khd->hqd', weights.astype(jnp.bfloat16), value_rows, pref...  7.34 us
  transfers between devices with their start and end apart: 7, of which 1 were waited for; matrix products, arithmetic and copies ran while one was open for 13% of the time, Pallas kernels for 0%

commit v1 on v0

v1 whole, which is shorter than its diff:
```python
import functools
import math

import jax
import jax.numpy as jnp
from jax import lax
from jax.experimental import pallas as pl
from jax.experimental.pallas import tpu as pltpu
from jax.sharding import PartitionSpec as P

HEADS = 24
HEAD_DIM = 128
FIXED_HEADS = 4
STRIDED_HEADS = 4
LOCAL_HEADS = 16
BLOCK = 128
LOOKBACK = 2
WIDTH = HEADS * HEAD_DIM

CHUNK_HEADS = 4
CHUNK = CHUNK_HEADS * HEAD_DIM
CHUNKS = HEADS // CHUNK_HEADS
FIXED_CHUNK = LOCAL_HEADS // CHUNK_HEADS
STRIDED_CHUNK = (LOCAL_HEADS + FIXED_HEADS) // CHUNK_HEADS
ORDER = tuple(range(FIXED_CHUNK)) + (STRIDED_CHUNK, FIXED_CHUNK)
FAR_ROWS = BLOCK + 16
FAR_COLS = 2 * CHUNK

NEG = -1e30
SCALE = math.log2(math.e) / math.sqrt(HEAD_DIM)
MESH = pl.DeviceIdType.MESH


def kernel(
    stride, groups, pos_ref, q_ref, k_ref, v_ref, keep_ref, o_ref,
    kcat, vcat, keeps, bias, st_src, st_buf, cur, rcv, fx_buf,
    halo_send, halo_recv, keep_send, keep_recv, ch_send, ch_recv,
    st_send, st_recv, fx_send, fx_recv,
):
    steps = stride.bit_length() - 1
    blocks = stride * groups
    window = lax.axis_index("grp")
    column = lax.axis_index("seq")
    me = window * stride + column
    odd = lax.rem(column, 2)
    is_odd = odd == 1
    is_even = odd == 0

    def device(block):
        return (lax.div(block, stride), lax.rem(block, stride))

    def partner(step):
        bit = 1 << step
        mine = lax.rem(lax.div(column, bit), 2)
        return (window, column + bit * (1 - 2 * mine))

    def cols(chunk):
        return pl.ds(chunk * CHUNK, CHUNK)

    barrier = pltpu.get_barrier_semaphore()
    greeted = 0
    for away in (-2, -1, 1, 2):
        there = (me + away >= 0) & (me + away < blocks)

        @pl.when(there)
        def _():
            pl.semaphore_signal(barrier, inc=1, device_id=device(me + away), device_id_type=MESH)

        greeted = greeted + there.astype(jnp.int32)
    for step in range(steps):
        pl.semaphore_signal(barrier, inc=1, device_id=partner(step), device_id_type=MESH)
    for away in range(1, groups):
        other = lax.rem(window + away, groups)
        pl.semaphore_signal(barrier, inc=1, device_id=(other, column), device_id_type=MESH)

    keep_row = keep_ref[...].astype(jnp.float32)
    keep_tile = jnp.broadcast_to(keep_row, (16, BLOCK)).astype(jnp.bfloat16)
    keeps[2] = keep_tile
    for buf, chunk in ((st_src, STRIDED_CHUNK), (cur.at[0], FIXED_CHUNK)):
        buf[0:BLOCK, 0:CHUNK] = k_ref[:, cols(chunk)]
        buf[0:BLOCK, CHUNK:FAR_COLS] = v_ref[:, cols(chunk)]
        for lane in range(0, FAR_COLS, BLOCK):
            buf[BLOCK:FAR_ROWS, lane : lane + BLOCK] = keep_tile

    pl.semaphore_wait(barrier, greeted + (steps + groups - 1))

    def keep_copy(ahead):
        slot = LOOKBACK - ahead
        return pltpu.make_async_remote_copy(
            src_ref=keeps.at[2], dst_ref=keeps.at[slot],
            send_sem=keep_send.at[slot], recv_sem=keep_recv.at[slot],
            device_id=device(jnp.minimum(me + ahead, blocks - 1)), device_id_type=MESH)

    def chain_copy(step):
        return pltpu.make_async_remote_copy(
            src_ref=cur.at[step], dst_ref=rcv.at[step],
            send_sem=ch_send.at[step], recv_sem=ch_recv.at[step],
            device_id=partner(step), device_id_type=MESH)

    def group_copy(src, buf, send_sem, recv_sem, away):
        return pltpu.make_async_remote_copy(
            src_ref=src, dst_ref=buf.at[window],
            send_sem=send_sem.at[away - 1], recv_sem=recv_sem.at[window],
            device_id=(window + away, column), device_id_type=MESH)

    def group_arrival(src, buf, send_sem, recv_sem, slot):
        return pltpu.make_async_remote_copy(
            src_ref=src, dst_ref=buf.at[slot],
            send_sem=send_sem.at[0], recv_sem=recv_sem.at[slot],
            device_id=(slot, column), device_id_type=MESH)

    def halo_copy(slot, part, chunk, src, target):
        cat = (kcat, vcat)[part]
        return pltpu.make_async_remote_copy(
            src_ref=src, dst_ref=cat.at[pl.ds(slot * BLOCK, BLOCK), cols(chunk)],
            send_sem=halo_send.at[slot, part, chunk], recv_sem=halo_recv.at[slot, part, chunk],
            device_id=device(target), device_id_type=MESH)

    def own(part, chunk):
        return (k_ref, v_ref)[part].at[:, cols(chunk)]

    def ahead_two(part, chunk):
        return halo_copy(0, part, chunk, own(part, chunk), me + 2)

    def ahead_one(part, chunk):
        return halo_copy(1, part, chunk, own(part, chunk), me + 1)

    def forward(part, chunk):
        src = (kcat, vcat)[part].at[pl.ds(0, BLOCK), cols(chunk)]
        return halo_copy(1, part, chunk, src, me - 1)

    has_two_ahead = me + 2 < blocks
    has_one_ahead = me + 1 < blocks
    has_two_back = me >= 2
    has_one_back = me >= 1
    forwards = is_odd & has_two_back

    @pl.when(has_one_ahead)
    def _():
        keep_copy(1).start()

    @pl.when(has_two_ahead)
    def _():
        keep_copy(2).start()

    chain_copy(0).start()
    for away in range(1, groups):

        @pl.when(window + away < groups)
        def _():
            group_copy(st_src, st_buf, st_send, st_recv, away).start()

    for chunk in ORDER:

        @pl.when(has_two_ahead)
        def _():
            for part in (0, 1):
                ahead_two(part, chunk).start()

        @pl.when(is_even)
        def _():
            for part in (0, 1):
                ahead_one(part, chunk).start()

    kcat[2 * BLOCK : 3 * BLOCK, :] = k_ref[...]
    vcat[2 * BLOCK : 3 * BLOCK, :] = v_ref[...]

    @pl.when(me < 2)
    def _():
        keeps[0] = jnp.zeros((16, BLOCK), jnp.bfloat16)
        kcat[0:BLOCK, :] = jnp.zeros((BLOCK, WIDTH), jnp.bfloat16)
        vcat[0:BLOCK, :] = jnp.zeros((BLOCK, WIDTH), jnp.bfloat16)

    @pl.when(me < 1)
    def _():
        keeps[1] = jnp.zeros((16, BLOCK), jnp.bfloat16)
        kcat[BLOCK : 2 * BLOCK, :] = jnp.zeros((BLOCK, WIDTH), jnp.bfloat16)
        vcat[BLOCK : 2 * BLOCK, :] = jnp.zeros((BLOCK, WIDTH), jnp.bfloat16)

    for slot in range(groups - 1):

        @pl.when(slot >= window)
        def _():
            st_buf[slot] = jnp.zeros((FAR_ROWS, FAR_COLS), jnp.bfloat16)
            fx_buf[slot] = jnp.zeros((FAR_ROWS, FAR_COLS), jnp.bfloat16)

    @pl.when(has_two_back)
    def _():
        keep_copy(2).wait_recv()

    @pl.when(has_one_back)
    def _():
        keep_copy(1).wait_recv()

    def as_bias(flags):
        return jnp.where(flags > 0.5, 0.0, NEG)

    for slot in (0, 1):
        row = as_bias(keeps[slot][0:1, :].astype(jnp.float32))
        bias[:, slot * BLOCK : (slot + 1) * BLOCK] = jnp.broadcast_to(row, (BLOCK, BLOCK))
    query_ids = lax.broadcasted_iota(jnp.int32, (BLOCK, BLOCK), 0)
    key_ids = lax.broadcasted_iota(jnp.int32, (BLOCK, BLOCK), 1)
    flags = jnp.where(key_ids == query_ids, 1.0, jnp.broadcast_to(keep_row, (BLOCK, BLOCK)))
    bias[:, 2 * BLOCK :] = as_bias(jnp.where(key_ids <= query_ids, flags, 0.0))

    def attend(chunk, far):
        rows = []
        for buf, flag in far:
            keep = buf[BLOCK : BLOCK + 16, 0:BLOCK].astype(jnp.float32)[0:1, :]
            rows.append(as_bias(keep * flag))
        for h in range(CHUNK_HEADS):
            at = chunk * CHUNK + h * HEAD_DIM
            head = pl.ds(at, HEAD_DIM)
            q = q_ref[:, head]
            nt = (((1,), (1,)), ((), ()))
            near = lax.dot_general(q, kcat[:, head], nt, preferred_element_type=jnp.float32)
            scores = [near * SCALE + bias[...]]
            for (buf, _), row in zip(far, rows):
                keys = buf[0:BLOCK, h * HEAD_DIM : (h + 1) * HEAD_DIM]
                term = lax.dot_general(q, keys, nt, preferred_element_type=jnp.float32)
                scores.append(term * SCALE + row)
            top = jnp.max(scores[0], axis=1, keepdims=True)
            for s in scores[1:]:
                top = jnp.maximum(top, jnp.max(s, axis=1, keepdims=True))
            total = 0.0
            weighted = 0.0
            for i, s in enumerate(scores):
                w = jnp.exp2(s - top)
                total = total + jnp.sum(w, axis=1, keepdims=True)
                if i == 0:
                    values = vcat[:, head]
                else:
                    values = far[i - 1][0][0:BLOCK, CHUNK + h * HEAD_DIM : CHUNK + (h + 1) * HEAD_DIM]
                weighted = weighted + jnp.dot(
                    w.astype(jnp.bfloat16), values, preferred_element_type=jnp.float32)
            o_ref[:, head] = (weighted / total).astype(jnp.bfloat16)

    def chain_step(step):
        chain_copy(step).wait_recv()
        bit = 1 << step
        theirs = lax.rem(lax.div(pos_ref[window], bit), 2)
        mine = lax.rem(lax.div(column, bit), 2)
        take = jnp.abs(theirs - mine).astype(jnp.float32)
        kept = cur[step].astype(jnp.float32) * (1.0 - take) + rcv[step].astype(jnp.float32) * take
        cur[step + 1] = kept.astype(jnp.bfloat16)
        if step + 1 < steps:
            chain_copy(step + 1).start()
        else:
            for away in range(1, groups):

                @pl.when(window + away < groups)
                def _():
                    group_copy(cur.at[steps], fx_buf, fx_send, fx_recv, away).start()

    for turn, chunk in enumerate(ORDER):
        if turn < steps:
            chain_step(turn)

        @pl.when(has_two_back)
        def _():
            for part in (0, 1):
                ahead_two(part, chunk).wait_recv()

        @pl.when(forwards)
        def _():
            for part in (0, 1):
                forward(part, chunk).start()

        @pl.when(has_one_back)
        def _():
            for part in (0, 1):
                ahead_one(part, chunk).wait_recv()

        far = []
        if chunk == STRIDED_CHUNK:
            for slot in range(groups - 1):

                @pl.when(slot < window)
                def _():
                    group_arrival(st_src, st_buf, st_send, st_recv, slot).wait_recv()

                far.append((st_buf.at[slot], (slot < window).astype(jnp.float32)))
        if chunk == FIXED_CHUNK:
            for slot in range(groups - 1):

                @pl.when(slot < window)
                def _():
                    group_arrival(st_src, fx_buf, fx_send, fx_recv, slot).wait_recv()

                used = (slot < window) & (slot * stride + pos_ref[slot] < me - LOOKBACK)
                far.append((fx_buf.at[slot], used.astype(jnp.float32)))
            used = window * stride + pos_ref[window] < me - LOOKBACK
            far.append((cur.at[steps], used.astype(jnp.float32)))
        attend(chunk, far)

    @pl.when(has_one_ahead)
    def _():
        keep_copy(1).wait_send()

    @pl.when(has_two_ahead)
    def _():
        keep_copy(2).wait_send()
        for chunk in ORDER:
            for part in (0, 1):
                ahead_two(part, chunk).wait_send()

    @pl.when(is_even | forwards)
    def _():
        for chunk in ORDER:
            for part in (0, 1):
                ahead_one(part, chunk).wait_send()

    for step in range(steps):
        chain_copy(step).wait_send()
    for away in range(1, groups):

        @pl.when(window + away < groups)
        def _():
            group_copy(st_src, st_buf, st_send, st_recv, away).wait_send()
            group_copy(cur.at[steps], fx_buf, fx_send, fx_recv, away).wait_send()


def on_device(queries, key_states, value_states, key_keep, summary_pos, *, stride, groups):
    steps = stride.bit_length() - 1
    assert 1 << steps == stride and steps < CHUNKS
    vmem = pl.BlockSpec(memory_space=pltpu.VMEM)
    dma = pltpu.SemaphoreType.DMA
    far = (FAR_ROWS, FAR_COLS)
    return pl.pallas_call(
        functools.partial(kernel, stride, groups),
        out_shape=jax.ShapeDtypeStruct((BLOCK, WIDTH), jnp.bfloat16),
        in_specs=[pl.BlockSpec(memory_space=pltpu.SMEM), vmem, vmem, vmem, vmem],
        out_specs=vmem,
        scratch_shapes=[
            pltpu.VMEM((3 * BLOCK, WIDTH), jnp.bfloat16),
            pltpu.VMEM((3 * BLOCK, WIDTH), jnp.bfloat16),
            pltpu.VMEM((3, 16, BLOCK), jnp.bfloat16),
            pltpu.VMEM((BLOCK, 3 * BLOCK), jnp.float32),
            pltpu.VMEM(far, jnp.bfloat16),
            pltpu.VMEM((groups - 1,) + far, jnp.bfloat16),
            pltpu.VMEM((steps + 1,) + far, jnp.bfloat16),
            pltpu.VMEM((steps,) + far, jnp.bfloat16),
            pltpu.VMEM((groups - 1,) + far, jnp.bfloat16),
            dma((2, 2, CHUNKS)), dma((2, 2, CHUNKS)),
            dma((2,)), dma((2,)),
            dma((steps,)), dma((steps,)),
            dma((groups - 1,)), dma((groups - 1,)),
            dma((groups - 1,)), dma((groups - 1,)),
        ],
        compiler_params=pltpu.CompilerParams(
            collective_id=0, has_side_effects=True, vmem_limit_bytes=40 * 1024 * 1024),
    )(summary_pos, queries, key_states, value_states, key_keep.reshape(1, BLOCK))


def solution(mesh):
    rows = P(("grp", "seq"), None)
    return jax.shard_map(
        functools.partial(on_device, stride=mesh.shape["seq"], groups=mesh.shape["grp"]),
        mesh=mesh,
        in_specs=(rows, rows, rows, P(("grp", "seq")), P()),
        out_specs=rows,
        check_vma=False,
    )
```

time: 177 us -> 91.4 us (0.52)
  the two profiles are of different devices: /device:TPU:3 before, /device:TPU:24 now
where the time goes in v1:
time: 91.4 us; the launch traced here: 91.1 us
  Pallas kernels  86.2 us (94%)
  local copies, waits for them, and re-layouts  4.95 us (5%)
    pallas_call x1, Pallas kernels, on_device(): pl.pallas_call(functools.partial(kernel, stride, groups), out_shape=jax.S...  86.2 us
    unnamed x11, local copies, waits for them, and re-layouts  4.95 us

profile of v1, /device:TPU:24, one launch (start us, length us, event | category | flops | bytes accessed | tf_op | source)
XLA Modules:
  0.0 91.1 jit_solution(13717786413994344933)
XLA Ops:
  0.0 0.0 copy-start.3
  0.0 0.0 copy-start.4
  0.0 0.7 copy-done.3
  0.7 0.0 copy-done.4
  0.7 0.0 copy-start
  0.7 1.1 %copy-done = bf16[128,3072]{1,0:T(8,128)(2,1)S(1)} copy-done((bf16[128,3072]{1,0:T(8,128)(2,1)S(1)}, bf16[128,3072]{1,0:T(8,128)(2,1)}, u32[]{:S(2)}) %copy-start) | copy-done | bytes 786456
  1.8 0.0 copy-start.1
  1.8 1.1 %copy-done.1 = bf16[128,3072]{1,0:T(8,128)(2,1)S(1)} copy-done((bf16[128,3072]{1,0:T(8,128)(2,1)S(1)}, bf16[128,3072]{1,0:T(8,128)(2,1)}, u32[]{:S(2)}) %copy-start.1) | copy-done | bytes 786456
  2.9 0.0 copy-start.2
  2.9 1.1 %copy-done.2 = bf16[128,3072]{1,0:T(8,128)(2,1)S(1)} copy-done((bf16[128,3072]{1,0:T(8,128)(2,1)S(1)}, bf16[128,3072]{1,0:T(8,128)(2,1)}, u32[]{:S(2)}) %copy-start.2) | copy-done | bytes 786456
  4.1 86.2 %shard_map.55 = bf16[128,3072]{1,0:T(8,128)(2,1)S(1)} custom-call(s32[4]{0:T(128)S(1)} %copy-done.3, bf16[128,3072]{1,0:T(8,128)(2,1)S(1)} %copy-done, bf16[128,3072]{1,0:T(8,128)(2,1)S(1)} %copy-done.1, bf16[128,3072]{1,0:T(8,128)(2,1)S(1)} %copy-done.2, s32[1,128]{1,0:T(1,128)S(1)} %bitcast.1), custom_call_target="tpu_custom_call" | custom-call | tf_op jit(solution)/shard_map/pallas_call | solution.py:329
  90.2 0.9 copy.7
Async XLA Ops:
  0.0 0.7 copy-start.3
  0.0 0.7 copy-start.4
  0.7 1.1 %copy-start = (bf16[128,3072]{1,0:T(8,128)(2,1)S(1)}, bf16[128,3072]{1,0:T(8,128)(2,1)}, u32[]{:S(2)}) copy-start(bf16[128,3072]{1,0:T(8,128)(2,1)} %q_ref.1) | copy-start | bytes 2359300
  1.8 1.1 %copy-start.1 = (bf16[128,3072]{1,0:T(8,128)(2,1)S(1)}, bf16[128,3072]{1,0:T(8,128)(2,1)}, u32[]{:S(2)}) copy-start(bf16[128,3072]{1,0:T(8,128)(2,1)} %k_ref.1) | copy-start | bytes 2359300
  2.9 1.1 %copy-start.2 = (bf16[128,3072]{1,0:T(8,128)(2,1)S(1)}, bf16[128,3072]{1,0:T(8,128)(2,1)}, u32[]{:S(2)}) copy-start(bf16[128,3072]{1,0:T(8,128)(2,1)} %v_ref.1) | copy-start | bytes 2359300

commit v2 on v1

--- a/solution.py
+++ b/solution.py
@@ -26,16 +26,17 @@
 FAR_ROWS = BLOCK + 16
 FAR_COLS = 2 * CHUNK
 
+AHEAD = 2
 NEG = -1e30
 SCALE = math.log2(math.e) / math.sqrt(HEAD_DIM)
 MESH = pl.DeviceIdType.MESH
 
 
 def kernel(
-    stride, groups, pos_ref, q_ref, k_ref, v_ref, keep_ref, o_ref,
-    kcat, vcat, keeps, bias, st_src, st_buf, cur, rcv, fx_buf,
+    stride, groups, pos_ref, q_hbm, k_hbm, v_hbm, keep_ref, o_ref,
+    q_ref, kcat, vcat, keeps, bias, st_src, st_buf, cur, rcv, fx_buf,
     halo_send, halo_recv, keep_send, keep_recv, ch_send, ch_recv,
-    st_send, st_recv, fx_send, fx_recv,
+    st_send, st_recv, st_pass, fx_send, fx_recv, fx_pass, load_sem,
 ):
     steps = stride.bit_length() - 1
     blocks = stride * groups
@@ -45,6 +46,16 @@
     odd = lax.rem(column, 2)
     is_odd = odd == 1
     is_even = odd == 0
+    core = lax.rem(window, 2)
+    chip = window - core
+    own_rows = pl.ds(LOOKBACK * BLOCK, BLOCK)
+    loads = [
+        pltpu.make_async_copy(src, dst, load_sem.at[i])
+        for i, (src, dst) in enumerate(
+            ((k_hbm, kcat.at[own_rows]), (v_hbm, vcat.at[own_rows]), (q_hbm, q_ref)))
+    ]
+    for load in loads:
+        load.start()
 
     def device(block):
         return (lax.div(block, stride), lax.rem(block, stride))
@@ -76,9 +87,11 @@
     keep_row = keep_ref[...].astype(jnp.float32)
     keep_tile = jnp.broadcast_to(keep_row, (16, BLOCK)).astype(jnp.bfloat16)
     keeps[2] = keep_tile
+    loads[0].wait()
+    loads[1].wait()
     for buf, chunk in ((st_src, STRIDED_CHUNK), (cur.at[0], FIXED_CHUNK)):
-        buf[0:BLOCK, 0:CHUNK] = k_ref[:, cols(chunk)]
-        buf[0:BLOCK, CHUNK:FAR_COLS] = v_ref[:, cols(chunk)]
+        buf[0:BLOCK, 0:CHUNK] = kcat[own_rows, cols(chunk)]
+        buf[0:BLOCK, CHUNK:FAR_COLS] = vcat[own_rows, cols(chunk)]
         for lane in range(0, FAR_COLS, BLOCK):
             buf[BLOCK:FAR_ROWS, lane : lane + BLOCK] = keep_tile
 
@@ -103,12 +116,6 @@
             send_sem=send_sem.at[away - 1], recv_sem=recv_sem.at[window],
             device_id=(window + away, column), device_id_type=MESH)
 
-    def group_arrival(src, buf, send_sem, recv_sem, slot):
-        return pltpu.make_async_remote_copy(
-            src_ref=src, dst_ref=buf.at[slot],
-            send_sem=send_sem.at[0], recv_sem=recv_sem.at[slot],
-            device_id=(slot, column), device_id_type=MESH)
-
     def halo_copy(slot, part, chunk, src, target):
         cat = (kcat, vcat)[part]
         return pltpu.make_async_remote_copy(
@@ -117,7 +124,7 @@
             device_id=device(target), device_id_type=MESH)
 
     def own(part, chunk):
-        return (k_ref, v_ref)[part].at[:, cols(chunk)]
+        return (kcat, vcat)[part].at[own_rows, cols(chunk)]
 
     def ahead_two(part, chunk):
         return halo_copy(0, part, chunk, own(part, chunk), me + 2)
@@ -143,14 +150,55 @@
     def _():
         keep_copy(2).start()
 
+    def goes(away):
+        if away == 1:
+            return core == 0
+        return (window + away < groups) & (away % 2 == 0)
+
+    def send_groups(src, buf, send_sem, recv_sem, act):
+        for away in range(1, groups):
+            if away == 1 or away % 2 == 0:
+
+                @pl.when(goes(away))
+                def _():
+                    act(group_copy(src, buf, send_sem, recv_sem, away))
+
+    def pass_copy(buf, recv_sem, pass_sem, slot):
+        return pltpu.make_async_remote_copy(
+            src_ref=buf.at[slot], dst_ref=buf.at[slot],
+            send_sem=pass_sem.at[slot], recv_sem=recv_sem.at[slot],
+            device_id=(chip + 1 - core, column), device_id_type=MESH)
+
+    def passes(slot):
+        return (slot < chip) & (core == slot % 2)
+
+    def pass_groups(buf, recv_sem, pass_sem):
+        for slot in range(groups - 2):
+
+            @pl.when(passes(slot))
+            def _():
+                copy = pass_copy(buf, recv_sem, pass_sem, slot)
+                copy.wait_recv()
+                copy.start()
+
+    def rest_of_groups(buf, recv_sem, pass_sem):
+        for slot in range(groups - 1):
+
+            @pl.when((slot < window) & jnp.logical_not(passes(slot)))
+            def _():
+                pass_copy(buf, recv_sem, pass_sem, slot).wait_recv()
+
+    def passed_on(buf, recv_sem, pass_sem):
+        for slot in range(groups - 2):
+
+            @pl.when(passes(slot))
+            def _():
+                pass_copy(buf, recv_sem, pass_sem, slot).wait_send()
+
     chain_copy(0).start()
-    for away in range(1, groups):
-
-        @pl.when(window + away < groups)
-        def _():
-            group_copy(st_src, st_buf, st_send, st_recv, away).start()
-
-    for chunk in ORDER:
+    send_groups(st_src, st_buf, st_send, st_recv, lambda copy: copy.start())
+
+    def send_chunk(chunk):
 
         @pl.when(has_two_ahead)
         def _():
@@ -162,8 +210,8 @@
             for part in (0, 1):
                 ahead_one(part, chunk).start()
 
-    kcat[2 * BLOCK : 3 * BLOCK, :] = k_ref[...]
-    vcat[2 * BLOCK : 3 * BLOCK, :] = v_ref[...]
+    for chunk in ORDER[:AHEAD]:
+        send_chunk(chunk)
 
     @pl.when(me < 2)
     def _():
@@ -246,25 +294,29 @@
         if step + 1 < steps:
             chain_copy(step + 1).start()
         else:
-            for away in range(1, groups):
-
-                @pl.when(window + away < groups)
-                def _():
-                    group_copy(cur.at[steps], fx_buf, fx_send, fx_recv, away).start()
-
+            send_groups(cur.at[steps], fx_buf, fx_send, fx_recv, lambda copy: copy.start())
+
+    loads[2].wait()
     for turn, chunk in enumerate(ORDER):
+
+        @pl.when(has_two_back)
+        def _():
+            for part in (0, 1):
+                ahead_two(part, chunk).wait_recv()
+
+        @pl.when(forwards)
+        def _():
+            for part in (0, 1):
+                forward(part, chunk).start()
+
         if turn < steps:
             chain_step(turn)
-
-        @pl.when(has_two_back)
-        def _():
-            for part in (0, 1):
-                ahead_two(part, chunk).wait_recv()
-
-        @pl.when(forwards)
-        def _():
-            for part in (0, 1):
-                forward(part, chunk).start()
+        if turn + AHEAD < CHUNKS:
+            send_chunk(ORDER[turn + AHEAD])
+        if turn == AHEAD:
+            pass_groups(st_buf, st_recv, st_pass)
+        if chunk == FIXED_CHUNK:
+            pass_groups(fx_buf, fx_recv, fx_pass)
 
         @pl.when(has_one_back)
         def _():
@@ -273,20 +325,12 @@
 
         far = []
         if chunk == STRIDED_CHUNK:
+            rest_of_groups(st_buf, st_recv, st_pass)
             for slot in range(groups - 1):
-
-                @pl.when(slot < window)
-                def _():
-                    group_arrival(st_src, st_buf, st_send, st_recv, slot).wait_recv()
-
                 far.append((st_buf.at[slot], (slot < window).astype(jnp.float32)))
         if chunk == FIXED_CHUNK:
+            rest_of_groups(fx_buf, fx_recv, fx_pass)
             for slot in range(groups - 1):
-
-                @pl.when(slot < window)
-                def _():
-                    group_arrival(st_src, fx_buf, fx_send, fx_recv, slot).wait_recv()
-
                 used = (slot < window) & (slot * stride + pos_ref[slot] < me - LOOKBACK)
                 far.append((fx_buf.at[slot], used.astype(jnp.float32)))
             used = window * stride + pos_ref[window] < me - LOOKBACK
@@ -312,26 +356,26 @@
 
     for step in range(steps):
         chain_copy(step).wait_send()
-    for away in range(1, groups):
-
-        @pl.when(window + away < groups)
-        def _():
-            group_copy(st_src, st_buf, st_send, st_recv, away).wait_send()
-            group_copy(cur.at[steps], fx_buf, fx_send, fx_recv, away).wait_send()
+    send_groups(st_src, st_buf, st_send, st_recv, lambda copy: copy.wait_send())
+    send_groups(cur.at[steps], fx_buf, fx_send, fx_recv, lambda copy: copy.wait_send())
+    passed_on(st_buf, st_recv, st_pass)
+    passed_on(fx_buf, fx_recv, fx_pass)
 
 
 def on_device(queries, key_states, value_states, key_keep, summary_pos, *, stride, groups):
     steps = stride.bit_length() - 1
-    assert 1 << steps == stride and steps < CHUNKS
+    assert 1 << steps == stride and steps < CHUNKS and groups % 2 == 0
     vmem = pl.BlockSpec(memory_space=pltpu.VMEM)
+    hbm = pl.BlockSpec(memory_space=pl.ANY)
     dma = pltpu.SemaphoreType.DMA
     far = (FAR_ROWS, FAR_COLS)
     return pl.pallas_call(
         functools.partial(kernel, stride, groups),
         out_shape=jax.ShapeDtypeStruct((BLOCK, WIDTH), jnp.bfloat16),
-        in_specs=[pl.BlockSpec(memory_space=pltpu.SMEM), vmem, vmem, vmem, vmem],
+        in_specs=[pl.BlockSpec(memory_space=pltpu.SMEM), hbm, hbm, hbm, vmem],
         out_specs=vmem,
         scratch_shapes=[
+            pltpu.VMEM((BLOCK, WIDTH), jnp.bfloat16),
             pltpu.VMEM((3 * BLOCK, WIDTH), jnp.bfloat16),
             pltpu.VMEM((3 * BLOCK, WIDTH), jnp.bfloat16),
             pltpu.VMEM((3, 16, BLOCK), jnp.bfloat16),
@@ -344,8 +388,9 @@
             dma((2, 2, CHUNKS)), dma((2, 2, CHUNKS)),
             dma((2,)), dma((2,)),
             dma((steps,)), dma((steps,)),
-            dma((groups - 1,)), dma((groups - 1,)),
-            dma((groups - 1,)), dma((groups - 1,)),
+            dma((groups - 1,)), dma((groups - 1,)), dma((groups - 1,)),
+            dma((groups - 1,)), dma((groups - 1,)), dma((groups - 1,)),
+            dma((3,)),
         ],
         compiler_params=pltpu.CompilerParams(
             collective_id=0, has_side_effects=True, vmem_limit_bytes=40 * 1024 * 1024),

time: 91.4 us -> 87.6 us (0.958)
  the two profiles are of different devices: /device:TPU:24 before, /device:TPU:8 now
where the time goes in v2:
time: 87.6 us; the launch traced here: 87.3 us
  Pallas kernels  82.4 us (94%)
  local copies, waits for them, and re-layouts  4.95 us (6%)
    pallas_call x1, Pallas kernels, on_device(): pl.pallas_call(functools.partial(kernel, stride, groups), out_shape=jax.S...  82.4 us
    unnamed x11, local copies, waits for them, and re-layouts  4.95 us

profile of v2, /device:TPU:8, one launch (start us, length us, event | category | flops | bytes accessed | tf_op | source)
XLA Modules:
  0.0 87.3 jit_solution(13851208444697617398)
XLA Ops:
  0.0 0.0 copy-start.3
  0.0 0.0 copy-start.4
  0.0 0.7 copy-done.3
  0.7 0.0 copy-done.4
  0.7 0.0 copy-start
  0.7 1.1 %copy-done = bf16[128,3072]{1,0:T(8,128)(2,1)S(1)} copy-done((bf16[128,3072]{1,0:T(8,128)(2,1)S(1)}, bf16[128,3072]{1,0:T(8,128)(2,1)}, u32[]{:S(2)}) %copy-start) | copy-done | bytes 786456
  1.8 0.0 copy-start.1
  1.8 1.1 %copy-done.1 = bf16[128,3072]{1,0:T(8,128)(2,1)S(1)} copy-done((bf16[128,3072]{1,0:T(8,128)(2,1)S(1)}, bf16[128,3072]{1,0:T(8,128)(2,1)}, u32[]{:S(2)}) %copy-start.1) | copy-done | bytes 786456
  2.9 0.0 copy-start.2
  2.9 1.1 %copy-done.2 = bf16[128,3072]{1,0:T(8,128)(2,1)S(1)} copy-done((bf16[128,3072]{1,0:T(8,128)(2,1)S(1)}, bf16[128,3072]{1,0:T(8,128)(2,1)}, u32[]{:S(2)}) %copy-start.2) | copy-done | bytes 786456
  4.1 82.4 %shard_map.55 = bf16[128,3072]{1,0:T(8,128)(2,1)S(1)} custom-call(s32[4]{0:T(128)S(1)} %copy-done.3, bf16[128,3072]{1,0:T(8,128)(2,1)S(1)} %copy-done, bf16[128,3072]{1,0:T(8,128)(2,1)S(1)} %copy-done.1, bf16[128,3072]{1,0:T(8,128)(2,1)S(1)} %copy-done.2, s32[1,128]{1,0:T(1,128)S(1)} %bitcast.1), custom_call_target="tpu_custom_call" | custom-call | tf_op jit(solution)/shard_map/pallas_call | solution.py:372
  86.5 0.9 %copy.7 = bf16[128,3072]{1,0:T(8,128)(2,1)} copy(bf16[128,3072]{1,0:T(8,128)(2,1)S(1)} %shard_map.55) | data formatting | bytes 1572864
Async XLA Ops:
  0.0 0.7 copy-start.3
  0.0 0.7 copy-start.4
  0.7 1.1 %copy-start = (bf16[128,3072]{1,0:T(8,128)(2,1)S(1)}, bf16[128,3072]{1,0:T(8,128)(2,1)}, u32[]{:S(2)}) copy-start(bf16[128,3072]{1,0:T(8,128)(2,1)} %q_hbm.1) | copy-start | bytes 2359300
  1.8 1.1 %copy-start.1 = (bf16[128,3072]{1,0:T(8,128)(2,1)S(1)}, bf16[128,3072]{1,0:T(8,128)(2,1)}, u32[]{:S(2)}) copy-start(bf16[128,3072]{1,0:T(8,128)(2,1)} %k_hbm.1) | copy-start | bytes 2359300
  2.9 1.1 %copy-start.2 = (bf16[128,3072]{1,0:T(8,128)(2,1)S(1)}, bf16[128,3072]{1,0:T(8,128)(2,1)}, u32[]{:S(2)}) copy-start(bf16[128,3072]{1,0:T(8,128)(2,1)} %v_hbm.1) | copy-start | bytes 2359300

commit v3 on v2

--- a/solution.py
+++ b/solution.py
@@ -25,6 +25,9 @@
 ORDER = tuple(range(FIXED_CHUNK)) + (STRIDED_CHUNK, FIXED_CHUNK)
 FAR_ROWS = BLOCK + 16
 FAR_COLS = 2 * CHUNK
+HALF = FAR_COLS // 2
+HALF_HEADS = CHUNK_HEADS // 2
+HALF_KEYS = HALF_HEADS * HEAD_DIM
 
 AHEAD = 2
 NEG = -1e30
@@ -34,7 +37,7 @@
 
 def kernel(
     stride, groups, pos_ref, q_hbm, k_hbm, v_hbm, keep_ref, o_ref,
-    q_ref, kcat, vcat, keeps, bias, st_src, st_buf, cur, rcv, fx_buf,
+    q_ref, kcat, vcat, keeps, bias, st_src, st_buf, fx_src, half, rcv, fin, fx_buf,
     halo_send, halo_recv, keep_send, keep_recv, ch_send, ch_recv,
     st_send, st_recv, st_pass, fx_send, fx_recv, fx_pass, load_sem,
 ):
@@ -89,9 +92,11 @@
     keeps[2] = keep_tile
     loads[0].wait()
     loads[1].wait()
-    for buf, chunk in ((st_src, STRIDED_CHUNK), (cur.at[0], FIXED_CHUNK)):
-        buf[0:BLOCK, 0:CHUNK] = kcat[own_rows, cols(chunk)]
-        buf[0:BLOCK, CHUNK:FAR_COLS] = vcat[own_rows, cols(chunk)]
+    for buf, chunk in ((st_src, STRIDED_CHUNK), (fx_src, FIXED_CHUNK)):
+        for i in (0, 1):
+            some = pl.ds(chunk * CHUNK + i * HALF_KEYS, HALF_KEYS)
+            buf[0:BLOCK, i * HALF : i * HALF + HALF_KEYS] = kcat[own_rows, some]
+            buf[0:BLOCK, i * HALF + HALF_KEYS : (i + 1) * HALF] = vcat[own_rows, some]
         for lane in range(0, FAR_COLS, BLOCK):
             buf[BLOCK:FAR_ROWS, lane : lane + BLOCK] = keep_tile
 
@@ -104,11 +109,20 @@
             send_sem=keep_send.at[slot], recv_sem=keep_recv.at[slot],
             device_id=device(jnp.minimum(me + ahead, blocks - 1)), device_id_type=MESH)
 
+    mine_half = pl.ds(pl.multiple_of(odd * HALF, HALF), HALF)
+    other_half = pl.ds(pl.multiple_of((1 - odd) * HALF, HALF), HALF)
+
     def chain_copy(step):
+        if step == 0:
+            src, dst = fx_src.at[:, other_half], rcv.at[0]
+        elif step < steps:
+            src, dst = half.at[step - 1], rcv.at[step]
+        else:
+            src, dst = fin.at[:, mine_half], fin.at[:, mine_half]
         return pltpu.make_async_remote_copy(
-            src_ref=cur.at[step], dst_ref=rcv.at[step],
+            src_ref=src, dst_ref=dst,
             send_sem=ch_send.at[step], recv_sem=ch_recv.at[step],
-            device_id=partner(step), device_id_type=MESH)
+            device_id=partner(step % steps), device_id_type=MESH)
 
     def group_copy(src, buf, send_sem, recv_sem, away):
         return pltpu.make_async_remote_copy(
@@ -259,12 +273,13 @@
         for h in range(CHUNK_HEADS):
             at = chunk * CHUNK + h * HEAD_DIM
             head = pl.ds(at, HEAD_DIM)
+            far_at = h // HALF_HEADS * HALF + h % HALF_HEADS * HEAD_DIM
             q = q_ref[:, head]
             nt = (((1,), (1,)), ((), ()))
             near = lax.dot_general(q, kcat[:, head], nt, preferred_element_type=jnp.float32)
             scores = [near * SCALE + bias[...]]
             for (buf, _), row in zip(far, rows):
-                keys = buf[0:BLOCK, h * HEAD_DIM : (h + 1) * HEAD_DIM]
+                keys = buf[0:BLOCK, far_at : far_at + HEAD_DIM]
                 term = lax.dot_general(q, keys, nt, preferred_element_type=jnp.float32)
                 scores.append(term * SCALE + row)
             top = jnp.max(scores[0], axis=1, keepdims=True)
@@ -278,23 +293,40 @@
                 if i == 0:
                     values = vcat[:, head]
                 else:
-                    values = far[i - 1][0][0:BLOCK, CHUNK + h * HEAD_DIM : CHUNK + (h + 1) * HEAD_DIM]
+                    far_values = far_at + HALF_KEYS
+                    values = far[i - 1][0][0:BLOCK, far_values : far_values + HEAD_DIM]
                 weighted = weighted + jnp.dot(
                     w.astype(jnp.bfloat16), values, preferred_element_type=jnp.float32)
             o_ref[:, head] = (weighted / total).astype(jnp.bfloat16)
 
     def chain_step(step):
         chain_copy(step).wait_recv()
+        if step == steps:
+            send_groups(fin, fx_buf, fx_send, fx_recv, lambda copy: copy.start())
+            return
         bit = 1 << step
         theirs = lax.rem(lax.div(pos_ref[window], bit), 2)
         mine = lax.rem(lax.div(column, bit), 2)
         take = jnp.abs(theirs - mine).astype(jnp.float32)
-        kept = cur[step].astype(jnp.float32) * (1.0 - take) + rcv[step].astype(jnp.float32) * take
-        cur[step + 1] = kept.astype(jnp.bfloat16)
+        held = fx_src[:, mine_half] if step == 0 else half[step - 1]
+        kept = held.astype(jnp.float32) * (1.0 - take) + rcv[step].astype(jnp.float32) * take
         if step + 1 < steps:
-            chain_copy(step + 1).start()
+            half[step] = kept.astype(jnp.bfloat16)
         else:
-            send_groups(cur.at[steps], fx_buf, fx_send, fx_recv, lambda copy: copy.start())
+            fin[:, mine_half] = kept.astype(jnp.bfloat16)
+        chain_copy(step + 1).start()
+
+    def own_sent(chunk):
+
+        @pl.when(has_two_ahead)
+        def _():
+            for part in (0, 1):
+                ahead_two(part, chunk).wait_send()
+
+        @pl.when(is_even)
+        def _():
+            for part in (0, 1):
+                ahead_one(part, chunk).wait_send()
 
     loads[2].wait()
     for turn, chunk in enumerate(ORDER):
@@ -309,9 +341,10 @@
             for part in (0, 1):
                 forward(part, chunk).start()
 
-        if turn < steps:
+        if turn <= steps:
             chain_step(turn)
         if turn + AHEAD < CHUNKS:
+            own_sent(chunk)
             send_chunk(ORDER[turn + AHEAD])
         if turn == AHEAD:
             pass_groups(st_buf, st_recv, st_pass)
@@ -334,7 +367,7 @@
                 used = (slot < window) & (slot * stride + pos_ref[slot] < me - LOOKBACK)
                 far.append((fx_buf.at[slot], used.astype(jnp.float32)))
             used = window * stride + pos_ref[window] < me - LOOKBACK
-            far.append((cur.at[steps], used.astype(jnp.float32)))
+            far.append((fin, used.astype(jnp.float32)))
         attend(chunk, far)
 
     @pl.when(has_one_ahead)
@@ -344,27 +377,27 @@
     @pl.when(has_two_ahead)
     def _():
         keep_copy(2).wait_send()
+
+    for chunk in ORDER[CHUNKS - AHEAD :]:
+        own_sent(chunk)
+
+    @pl.when(forwards)
+    def _():
         for chunk in ORDER:
             for part in (0, 1):
-                ahead_two(part, chunk).wait_send()
-
-    @pl.when(is_even | forwards)
-    def _():
-        for chunk in ORDER:
-            for part in (0, 1):
-                ahead_one(part, chunk).wait_send()
-
-    for step in range(steps):
+                forward(part, chunk).wait_send()
+
+    for step in range(steps + 1):
         chain_copy(step).wait_send()
     send_groups(st_src, st_buf, st_send, st_recv, lambda copy: copy.wait_send())
-    send_groups(cur.at[steps], fx_buf, fx_send, fx_recv, lambda copy: copy.wait_send())
+    send_groups(fin, fx_buf, fx_send, fx_recv, lambda copy: copy.wait_send())
     passed_on(st_buf, st_recv, st_pass)
     passed_on(fx_buf, fx_recv, fx_pass)
 
 
 def on_device(queries, key_states, value_states, key_keep, summary_pos, *, stride, groups):
     steps = stride.bit_length() - 1
-    assert 1 << steps == stride and steps < CHUNKS and groups % 2 == 0
+    assert 1 << steps == stride and 1 < steps < CHUNKS and groups % 2 == 0
     vmem = pl.BlockSpec(memory_space=pltpu.VMEM)
     hbm = pl.BlockSpec(memory_space=pl.ANY)
     dma = pltpu.SemaphoreType.DMA
@@ -382,12 +415,14 @@
             pltpu.VMEM((BLOCK, 3 * BLOCK), jnp.float32),
             pltpu.VMEM(far, jnp.bfloat16),
             pltpu.VMEM((groups - 1,) + far, jnp.bfloat16),
-            pltpu.VMEM((steps + 1,) + far, jnp.bfloat16),
-            pltpu.VMEM((steps,) + far, jnp.bfloat16),
+            pltpu.VMEM(far, jnp.bfloat16),
+            pltpu.VMEM((steps - 1, FAR_ROWS, HALF), jnp.bfloat16),
+            pltpu.VMEM((steps, FAR_ROWS, HALF), jnp.bfloat16),
+            pltpu.VMEM(far, jnp.bfloat16),
             pltpu.VMEM((groups - 1,) + far, jnp.bfloat16),
             dma((2, 2, CHUNKS)), dma((2, 2, CHUNKS)),
             dma((2,)), dma((2,)),
-            dma((steps,)), dma((steps,)),
+            dma((steps + 1,)), dma((steps + 1,)),
             dma((groups - 1,)), dma((groups - 1,)), dma((groups - 1,)),
             dma((groups - 1,)), dma((groups - 1,)), dma((groups - 1,)),
             dma((3,)),

time: 87.6 us -> 78.1 us (0.89)
  Pallas kernels: 82.4 us -> 72.8 us
    pallas_call x1, Pallas kernels: 82.4 us -> 72.8 us  [on_device(): pl.pallas_call(functools.partial(kernel, stride, groups), out_shape=jax.S...]
where the time goes in v3:
time: 78.1 us; the launch traced here: 77.8 us
  Pallas kernels  72.8 us (93%)
  local copies, waits for them, and re-layouts  4.95 us (6%)
    pallas_call x1, Pallas kernels, on_device(): pl.pallas_call(functools.partial(kernel, stride, groups), out_shape=jax.S...  72.8 us
    unnamed x11, local copies, waits for them, and re-layouts  4.95 us

profile of v3, /device:TPU:8, one launch (start us, length us, event | category | flops | bytes accessed | tf_op | source)
XLA Modules:
  0.0 77.8 jit_solution(860816601201848729)
XLA Ops:
  0.0 0.0 copy-start.3
  0.0 0.0 copy-start.4
  0.0 0.7 copy-done.3
  0.7 0.0 copy-done.4
  0.7 0.0 copy-start
  0.7 1.1 %copy-done = bf16[128,3072]{1,0:T(8,128)(2,1)S(1)} copy-done((bf16[128,3072]{1,0:T(8,128)(2,1)S(1)}, bf16[128,3072]{1,0:T(8,128)(2,1)}, u32[]{:S(2)}) %copy-start) | copy-done | bytes 786456
  1.8 0.0 copy-start.1
  1.8 1.1 %copy-done.1 = bf16[128,3072]{1,0:T(8,128)(2,1)S(1)} copy-done((bf16[128,3072]{1,0:T(8,128)(2,1)S(1)}, bf16[128,3072]{1,0:T(8,128)(2,1)}, u32[]{:S(2)}) %copy-start.1) | copy-done | bytes 786456
  2.9 0.0 copy-start.2
  2.9 1.1 %copy-done.2 = bf16[128,3072]{1,0:T(8,128)(2,1)S(1)} copy-done((bf16[128,3072]{1,0:T(8,128)(2,1)S(1)}, bf16[128,3072]{1,0:T(8,128)(2,1)}, u32[]{:S(2)}) %copy-start.2) | copy-done | bytes 786456
  4.1 72.8 %shard_map.55 = bf16[128,3072]{1,0:T(8,128)(2,1)S(1)} custom-call(s32[4]{0:T(128)S(1)} %copy-done.3, bf16[128,3072]{1,0:T(8,128)(2,1)S(1)} %copy-done, bf16[128,3072]{1,0:T(8,128)(2,1)S(1)} %copy-done.1, bf16[128,3072]{1,0:T(8,128)(2,1)S(1)} %copy-done.2, s32[1,128]{1,0:T(1,128)S(1)} %bitcast.1), custom_call_target="tpu_custom_call" | custom-call | tf_op jit(solution)/shard_map/pallas_call | solution.py:405
  76.9 0.9 %copy.7 = bf16[128,3072]{1,0:T(8,128)(2,1)} copy(bf16[128,3072]{1,0:T(8,128)(2,1)S(1)} %shard_map.55) | data formatting | bytes 1572864
Async XLA Ops:
  0.0 0.7 copy-start.3
  0.0 0.7 copy-start.4
  0.7 1.1 %copy-start = (bf16[128,3072]{1,0:T(8,128)(2,1)S(1)}, bf16[128,3072]{1,0:T(8,128)(2,1)}, u32[]{:S(2)}) copy-start(bf16[128,3072]{1,0:T(8,128)(2,1)} %q_hbm.1) | copy-start | bytes 2359300
  1.8 1.1 %copy-start.1 = (bf16[128,3072]{1,0:T(8,128)(2,1)S(1)}, bf16[128,3072]{1,0:T(8,128)(2,1)}, u32[]{:S(2)}) copy-start(bf16[128,3072]{1,0:T(8,128)(2,1)} %k_hbm.1) | copy-start | bytes 2359300
  2.9 1.1 %copy-start.2 = (bf16[128,3072]{1,0:T(8,128)(2,1)S(1)}, bf16[128,3072]{1,0:T(8,128)(2,1)}, u32[]{:S(2)}) copy-start(bf16[128,3072]{1,0:T(8,128)(2,1)} %v_hbm.1) | copy-start | bytes 2359300

commit v4 on v3

--- a/solution.py
+++ b/solution.py
@@ -330,22 +330,22 @@
 
     loads[2].wait()
     for turn, chunk in enumerate(ORDER):
-
-        @pl.when(has_two_back)
-        def _():
-            for part in (0, 1):
-                ahead_two(part, chunk).wait_recv()
-
-        @pl.when(forwards)
-        def _():
-            for part in (0, 1):
-                forward(part, chunk).start()
-
-        if turn <= steps:
-            chain_step(turn)
         if turn + AHEAD < CHUNKS:
             own_sent(chunk)
             send_chunk(ORDER[turn + AHEAD])
+
+        @pl.when(has_two_back)
+        def _():
+            for part in (0, 1):
+                ahead_two(part, chunk).wait_recv()
+
+        @pl.when(forwards)
+        def _():
+            for part in (0, 1):
+                forward(part, chunk).start()
+
+        if steps == CHUNKS - 1 == turn:
+            chain_step(turn)
         if turn == AHEAD:
             pass_groups(st_buf, st_recv, st_pass)
         if chunk == FIXED_CHUNK:
@@ -368,6 +368,8 @@
                 far.append((fx_buf.at[slot], used.astype(jnp.float32)))
             used = window * stride + pos_ref[window] < me - LOOKBACK
             far.append((fin, used.astype(jnp.float32)))
+        if turn <= steps and turn < CHUNKS - 1:
+            chain_step(turn)
         attend(chunk, far)
 
     @pl.when(has_one_ahead)

time: 78.1 us -> 73.6 us (0.942)
  the two profiles are of different devices: /device:TPU:8 before, /device:TPU:3 now
where the time goes in v4:
time: 73.6 us; the launch traced here: 72.7 us
  Pallas kernels  67.8 us (92%)
  local copies, waits for them, and re-layouts  4.95 us (7%)
    pallas_call x1, Pallas kernels, on_device(): pl.pallas_call(functools.partial(kernel, stride, groups), out_shape=jax.S...  67.8 us
    unnamed x11, local copies, waits for them, and re-layouts  4.95 us

profile of v4, /device:TPU:3, one launch (start us, length us, event | category | flops | bytes accessed | tf_op | source)
XLA Modules:
  0.0 72.7 jit_solution(8440085710202059728)
XLA Ops:
  0.0 0.0 copy-start.3
  0.0 0.0 copy-start.4
  0.0 0.7 copy-done.3
  0.7 0.0 copy-done.4
  0.7 0.0 copy-start
  0.7 1.1 %copy-done = bf16[128,3072]{1,0:T(8,128)(2,1)S(1)} copy-done((bf16[128,3072]{1,0:T(8,128)(2,1)S(1)}, bf16[128,3072]{1,0:T(8,128)(2,1)}, u32[]{:S(2)}) %copy-start) | copy-done | bytes 786456
  1.8 0.0 copy-start.1
  1.8 1.1 %copy-done.1 = bf16[128,3072]{1,0:T(8,128)(2,1)S(1)} copy-done((bf16[128,3072]{1,0:T(8,128)(2,1)S(1)}, bf16[128,3072]{1,0:T(8,128)(2,1)}, u32[]{:S(2)}) %copy-start.1) | copy-done | bytes 786456
  2.9 0.0 copy-start.2
  2.9 1.1 %copy-done.2 = bf16[128,3072]{1,0:T(8,128)(2,1)S(1)} copy-done((bf16[128,3072]{1,0:T(8,128)(2,1)S(1)}, bf16[128,3072]{1,0:T(8,128)(2,1)}, u32[]{:S(2)}) %copy-start.2) | copy-done | bytes 786456
  4.1 67.8 %shard_map.55 = bf16[128,3072]{1,0:T(8,128)(2,1)S(1)} custom-call(s32[4]{0:T(128)S(1)} %copy-done.3, bf16[128,3072]{1,0:T(8,128)(2,1)S(1)} %copy-done, bf16[128,3072]{1,0:T(8,128)(2,1)S(1)} %copy-done.1, bf16[128,3072]{1,0:T(8,128)(2,1)S(1)} %copy-done.2, s32[1,128]{1,0:T(1,128)S(1)} %bitcast.1), custom_call_target="tpu_custom_call" | custom-call | tf_op jit(solution)/shard_map/pallas_call | solution.py:407
  71.9 0.9 %copy.7 = bf16[128,3072]{1,0:T(8,128)(2,1)} copy(bf16[128,3072]{1,0:T(8,128)(2,1)S(1)} %shard_map.55) | data formatting | bytes 1572864
Async XLA Ops:
  0.0 0.7 copy-start.3
  0.0 0.7 copy-start.4
  0.7 1.1 %copy-start = (bf16[128,3072]{1,0:T(8,128)(2,1)S(1)}, bf16[128,3072]{1,0:T(8,128)(2,1)}, u32[]{:S(2)}) copy-start(bf16[128,3072]{1,0:T(8,128)(2,1)} %q_hbm.1) | copy-start | bytes 2359300
  1.8 1.1 %copy-start.1 = (bf16[128,3072]{1,0:T(8,128)(2,1)S(1)}, bf16[128,3072]{1,0:T(8,128)(2,1)}, u32[]{:S(2)}) copy-start(bf16[128,3072]{1,0:T(8,128)(2,1)} %k_hbm.1) | copy-start | bytes 2359300
  2.9 1.1 %copy-start.2 = (bf16[128,3072]{1,0:T(8,128)(2,1)S(1)}, bf16[128,3072]{1,0:T(8,128)(2,1)}, u32[]{:S(2)}) copy-start(bf16[128,3072]{1,0:T(8,128)(2,1)} %v_hbm.1) | copy-start | bytes 2359300

commit v5 on v4

--- a/solution.py
+++ b/solution.py
@@ -17,19 +17,20 @@
 LOOKBACK = 2
 WIDTH = HEADS * HEAD_DIM
 
-CHUNK_HEADS = 4
+CHUNK_HEADS = 2
 CHUNK = CHUNK_HEADS * HEAD_DIM
 CHUNKS = HEADS // CHUNK_HEADS
 FIXED_CHUNK = LOCAL_HEADS // CHUNK_HEADS
 STRIDED_CHUNK = (LOCAL_HEADS + FIXED_HEADS) // CHUNK_HEADS
-ORDER = tuple(range(FIXED_CHUNK)) + (STRIDED_CHUNK, FIXED_CHUNK)
+ORDER = tuple(range(FIXED_CHUNK)) + tuple(range(STRIDED_CHUNK, CHUNKS)) + tuple(range(FIXED_CHUNK, STRIDED_CHUNK))
+FAR_HEADS = 4
 FAR_ROWS = BLOCK + 16
-FAR_COLS = 2 * CHUNK
+FAR_COLS = 2 * FAR_HEADS * HEAD_DIM
 HALF = FAR_COLS // 2
-HALF_HEADS = CHUNK_HEADS // 2
+HALF_HEADS = FAR_HEADS // 2
 HALF_KEYS = HALF_HEADS * HEAD_DIM
 
-AHEAD = 2
+AHEAD = 3
 NEG = -1e30
 SCALE = math.log2(math.e) / math.sqrt(HEAD_DIM)
 MESH = pl.DeviceIdType.MESH
@@ -92,9 +93,9 @@
     keeps[2] = keep_tile
     loads[0].wait()
     loads[1].wait()
-    for buf, chunk in ((st_src, STRIDED_CHUNK), (fx_src, FIXED_CHUNK)):
+    for buf, first in ((st_src, LOCAL_HEADS + FIXED_HEADS), (fx_src, LOCAL_HEADS)):
         for i in (0, 1):
-            some = pl.ds(chunk * CHUNK + i * HALF_KEYS, HALF_KEYS)
+            some = pl.ds(first * HEAD_DIM + i * HALF_KEYS, HALF_KEYS)
             buf[0:BLOCK, i * HALF : i * HALF + HALF_KEYS] = kcat[own_rows, some]
             buf[0:BLOCK, i * HALF + HALF_KEYS : (i + 1) * HALF] = vcat[own_rows, some]
         for lane in range(0, FAR_COLS, BLOCK):
@@ -273,7 +274,8 @@
         for h in range(CHUNK_HEADS):
             at = chunk * CHUNK + h * HEAD_DIM
             head = pl.ds(at, HEAD_DIM)
-            far_at = h // HALF_HEADS * HALF + h % HALF_HEADS * HEAD_DIM
+            far_head = (chunk * CHUNK_HEADS + h - LOCAL_HEADS) % FAR_HEADS
+            far_at = far_head // HALF_HEADS * HALF + far_head % HALF_HEADS * HEAD_DIM
             q = q_ref[:, head]
             nt = (((1,), (1,)), ((), ()))
             near = lax.dot_general(q, kcat[:, head], nt, preferred_element_type=jnp.float32)
@@ -329,6 +331,7 @@
                 ahead_one(part, chunk).wait_send()
 
     loads[2].wait()
+    spacing = 2 if 2 * steps + 1 < ORDER.index(FIXED_CHUNK) else 1
     for turn, chunk in enumerate(ORDER):
         if turn + AHEAD < CHUNKS:
             own_sent(chunk)
@@ -344,9 +347,7 @@
             for part in (0, 1):
                 forward(part, chunk).start()
 
-        if steps == CHUNKS - 1 == turn:
-            chain_step(turn)
-        if turn == AHEAD:
+        if turn == CHUNKS // 3:
             pass_groups(st_buf, st_recv, st_pass)
         if chunk == FIXED_CHUNK:
             pass_groups(fx_buf, fx_recv, fx_pass)
@@ -359,17 +360,19 @@
         far = []
         if chunk == STRIDED_CHUNK:
             rest_of_groups(st_buf, st_recv, st_pass)
+        if chunk >= STRIDED_CHUNK:
             for slot in range(groups - 1):
                 far.append((st_buf.at[slot], (slot < window).astype(jnp.float32)))
         if chunk == FIXED_CHUNK:
             rest_of_groups(fx_buf, fx_recv, fx_pass)
+        if FIXED_CHUNK <= chunk < STRIDED_CHUNK:
             for slot in range(groups - 1):
                 used = (slot < window) & (slot * stride + pos_ref[slot] < me - LOOKBACK)
                 far.append((fx_buf.at[slot], used.astype(jnp.float32)))
             used = window * stride + pos_ref[window] < me - LOOKBACK
             far.append((fin, used.astype(jnp.float32)))
-        if turn <= steps and turn < CHUNKS - 1:
-            chain_step(turn)
+        if turn % spacing == 1 % spacing and turn // spacing <= steps:
+            chain_step(turn // spacing)
         attend(chunk, far)
 
     @pl.when(has_one_ahead)
@@ -399,7 +402,7 @@
 
 def on_device(queries, key_states, value_states, key_keep, summary_pos, *, stride, groups):
     steps = stride.bit_length() - 1
-    assert 1 << steps == stride and 1 < steps < CHUNKS and groups % 2 == 0
+    assert 1 << steps == stride and 1 < steps < FIXED_CHUNK and groups % 2 == 0
     vmem = pl.BlockSpec(memory_space=pltpu.VMEM)
     hbm = pl.BlockSpec(memory_space=pl.ANY)
     dma = pltpu.SemaphoreType.DMA

time: 73.6 us -> 76.2 us (1.035)
  Pallas kernels: 67.8 us -> 71 us
    pallas_call x1, Pallas kernels: 67.8 us -> 71 us  [on_device(): pl.pallas_call(functools.partial(kernel, stride, groups), out_shape=jax.S...]
where the time goes in v5:
time: 76.2 us; the launch traced here: 75.9 us
  Pallas kernels  71 us (93%)
  local copies, waits for them, and re-layouts  4.95 us (6%)
    pallas_call x1, Pallas kernels, on_device(): pl.pallas_call(functools.partial(kernel, stride, groups), out_shape=jax.S...  71 us
    unnamed x11, local copies, waits for them, and re-layouts  4.95 us

profile of v5, /device:TPU:3, one launch (start us, length us, event | category | flops | bytes accessed | tf_op | source)
XLA Modules:
  0.0 75.9 jit_solution(9208738779393560181)
XLA Ops:
  0.0 0.0 copy-start.3
  0.0 0.0 copy-start.4
  0.0 0.7 copy-done.3
  0.7 0.0 copy-done.4
  0.7 0.0 copy-start
  0.7 1.1 %copy-done = bf16[128,3072]{1,0:T(8,128)(2,1)S(1)} copy-done((bf16[128,3072]{1,0:T(8,128)(2,1)S(1)}, bf16[128,3072]{1,0:T(8,128)(2,1)}, u32[]{:S(2)}) %copy-start) | copy-done | bytes 786456
  1.8 0.0 copy-start.1
  1.8 1.1 %copy-done.1 = bf16[128,3072]{1,0:T(8,128)(2,1)S(1)} copy-done((bf16[128,3072]{1,0:T(8,128)(2,1)S(1)}, bf16[128,3072]{1,0:T(8,128)(2,1)}, u32[]{:S(2)}) %copy-start.1) | copy-done | bytes 786456
  2.9 0.0 copy-start.2
  2.9 1.1 %copy-done.2 = bf16[128,3072]{1,0:T(8,128)(2,1)S(1)} copy-done((bf16[128,3072]{1,0:T(8,128)(2,1)S(1)}, bf16[128,3072]{1,0:T(8,128)(2,1)}, u32[]{:S(2)}) %copy-start.2) | copy-done | bytes 786456
  4.1 71.0 %shard_map.55 = bf16[128,3072]{1,0:T(8,128)(2,1)S(1)} custom-call(s32[4]{0:T(128)S(1)} %copy-done.3, bf16[128,3072]{1,0:T(8,128)(2,1)S(1)} %copy-done, bf16[128,3072]{1,0:T(8,128)(2,1)S(1)} %copy-done.1, bf16[128,3072]{1,0:T(8,128)(2,1)S(1)} %copy-done.2, s32[1,128]{1,0:T(1,128)S(1)} %bitcast.1), custom_call_target="tpu_custom_call" | custom-call | tf_op jit(solution)/shard_map/pallas_call | solution.py:410
  75.1 0.9 %copy.7 = bf16[128,3072]{1,0:T(8,128)(2,1)} copy(bf16[128,3072]{1,0:T(8,128)(2,1)S(1)} %shard_map.55) | data formatting | bytes 1572864
Async XLA Ops:
  0.0 0.7 copy-start.3
  0.0 0.7 copy-start.4
  0.7 1.1 %copy-start = (bf16[128,3072]{1,0:T(8,128)(2,1)S(1)}, bf16[128,3072]{1,0:T(8,128)(2,1)}, u32[]{:S(2)}) copy-start(bf16[128,3072]{1,0:T(8,128)(2,1)} %q_hbm.1) | copy-start | bytes 2359300
  1.8 1.1 %copy-start.1 = (bf16[128,3072]{1,0:T(8,128)(2,1)S(1)}, bf16[128,3072]{1,0:T(8,128)(2,1)}, u32[]{:S(2)}) copy-start(bf16[128,3072]{1,0:T(8,128)(2,1)} %k_hbm.1) | copy-start | bytes 2359300
  2.9 1.1 %copy-start.2 = (bf16[128,3072]{1,0:T(8,128)(2,1)S(1)}, bf16[128,3072]{1,0:T(8,128)(2,1)}, u32[]{:S(2)}) copy-start(bf16[128,3072]{1,0:T(8,128)(2,1)} %v_hbm.1) | copy-start | bytes 2359300

commit v6 on v5

--- a/solution.py
+++ b/solution.py
@@ -30,7 +30,7 @@
 HALF_HEADS = FAR_HEADS // 2
 HALF_KEYS = HALF_HEADS * HEAD_DIM
 
-AHEAD = 3
+AHEAD = 4
 NEG = -1e30
 SCALE = math.log2(math.e) / math.sqrt(HEAD_DIM)
 MESH = pl.DeviceIdType.MESH

time: 76.2 us -> 76.2 us (level)
  no operation moved by 1% of the time
where the time goes in v6:
time: 76.2 us; the launch traced here: 76 us
  Pallas kernels  71 us (93%)
  local copies, waits for them, and re-layouts  4.95 us (6%)
    pallas_call x1, Pallas kernels, on_device(): pl.pallas_call(functools.partial(kernel, stride, groups), out_shape=jax.S...  71 us
    unnamed x11, local copies, waits for them, and re-layouts  4.95 us

profile of v6, /device:TPU:3, one launch (start us, length us, event | category | flops | bytes accessed | tf_op | source)
XLA Modules:
  0.0 76.0 jit_solution(4138953092805264422)
XLA Ops:
  0.0 0.0 copy-start.3
  0.0 0.0 copy-start.4
  0.0 0.7 copy-done.3
  0.7 0.0 copy-done.4
  0.7 0.0 copy-start
  0.7 1.1 %copy-done = bf16[128,3072]{1,0:T(8,128)(2,1)S(1)} copy-done((bf16[128,3072]{1,0:T(8,128)(2,1)S(1)}, bf16[128,3072]{1,0:T(8,128)(2,1)}, u32[]{:S(2)}) %copy-start) | copy-done | bytes 786456
  1.8 0.0 copy-start.1
  1.8 1.1 %copy-done.1 = bf16[128,3072]{1,0:T(8,128)(2,1)S(1)} copy-done((bf16[128,3072]{1,0:T(8,128)(2,1)S(1)}, bf16[128,3072]{1,0:T(8,128)(2,1)}, u32[]{:S(2)}) %copy-start.1) | copy-done | bytes 786456
  2.9 0.0 copy-start.2
  2.9 1.1 %copy-done.2 = bf16[128,3072]{1,0:T(8,128)(2,1)S(1)} copy-done((bf16[128,3072]{1,0:T(8,128)(2,1)S(1)}, bf16[128,3072]{1,0:T(8,128)(2,1)}, u32[]{:S(2)}) %copy-start.2) | copy-done | bytes 786456
  4.1 71.0 %shard_map.55 = bf16[128,3072]{1,0:T(8,128)(2,1)S(1)} custom-call(s32[4]{0:T(128)S(1)} %copy-done.3, bf16[128,3072]{1,0:T(8,128)(2,1)S(1)} %copy-done, bf16[128,3072]{1,0:T(8,128)(2,1)S(1)} %copy-done.1, bf16[128,3072]{1,0:T(8,128)(2,1)S(1)} %copy-done.2, s32[1,128]{1,0:T(1,128)S(1)} %bitcast.1), custom_call_target="tpu_custom_call" | custom-call | tf_op jit(solution)/shard_map/pallas_call | solution.py:410
  75.1 0.9 %copy.7 = bf16[128,3072]{1,0:T(8,128)(2,1)} copy(bf16[128,3072]{1,0:T(8,128)(2,1)S(1)} %shard_map.55) | data formatting | bytes 1572864
Async XLA Ops:
  0.0 0.7 copy-start.3
  0.0 0.7 copy-start.4
  0.7 1.1 %copy-start = (bf16[128,3072]{1,0:T(8,128)(2,1)S(1)}, bf16[128,3072]{1,0:T(8,128)(2,1)}, u32[]{:S(2)}) copy-start(bf16[128,3072]{1,0:T(8,128)(2,1)} %q_hbm.1) | copy-start | bytes 2359300
  1.8 1.1 %copy-start.1 = (bf16[128,3072]{1,0:T(8,128)(2,1)S(1)}, bf16[128,3072]{1,0:T(8,128)(2,1)}, u32[]{:S(2)}) copy-start(bf16[128,3072]{1,0:T(8,128)(2,1)} %k_hbm.1) | copy-start | bytes 2359300
  2.9 1.1 %copy-start.2 = (bf16[128,3072]{1,0:T(8,128)(2,1)S(1)}, bf16[128,3072]{1,0:T(8,128)(2,1)}, u32[]{:S(2)}) copy-start(bf16[128,3072]{1,0:T(8,128)(2,1)} %v_hbm.1) | copy-start | bytes 2359300

commit v7 on v4

--- a/solution.py
+++ b/solution.py
@@ -316,9 +316,11 @@
             fin[:, mine_half] = kept.astype(jnp.bfloat16)
         chain_copy(step + 1).start()
 
+    crosses = column >= stride - LOOKBACK
+
     def own_sent(chunk):
 
-        @pl.when(has_two_ahead)
+        @pl.when(has_two_ahead & jnp.logical_not(crosses))
         def _():
             for part in (0, 1):
                 ahead_two(part, chunk).wait_send()
@@ -382,6 +384,12 @@
 
     for chunk in ORDER[CHUNKS - AHEAD :]:
         own_sent(chunk)
+
+    @pl.when(has_two_ahead & crosses)
+    def _():
+        for chunk in ORDER:
+            for part in (0, 1):
+                ahead_two(part, chunk).wait_send()
 
     @pl.when(forwards)
     def _():

time: 73.6 us -> 73.6 us (level)
  no operation moved by 1% of the time
where the time goes in v7:
time: 73.6 us; the launch traced here: 72.8 us
  Pallas kernels  67.8 us (92%)
  local copies, waits for them, and re-layouts  4.95 us (7%)
    pallas_call x1, Pallas kernels, on_device(): pl.pallas_call(functools.partial(kernel, stride, groups), out_shape=jax.S...  67.8 us
    unnamed x11, local copies, waits for them, and re-layouts  4.95 us

profile of v7, /device:TPU:3, one launch (start us, length us, event | category | flops | bytes accessed | tf_op | source)
XLA Modules:
  0.0 72.8 jit_solution(14073683538477928641)
XLA Ops:
  0.0 0.0 copy-start.3
  0.0 0.0 copy-start.4
  0.0 0.7 copy-done.3
  0.7 0.0 copy-done.4
  0.7 0.0 copy-start
  0.7 1.1 %copy-done = bf16[128,3072]{1,0:T(8,128)(2,1)S(1)} copy-done((bf16[128,3072]{1,0:T(8,128)(2,1)S(1)}, bf16[128,3072]{1,0:T(8,128)(2,1)}, u32[]{:S(2)}) %copy-start) | copy-done | bytes 786456
  1.8 0.0 copy-start.1
  1.8 1.1 %copy-done.1 = bf16[128,3072]{1,0:T(8,128)(2,1)S(1)} copy-done((bf16[128,3072]{1,0:T(8,128)(2,1)S(1)}, bf16[128,3072]{1,0:T(8,128)(2,1)}, u32[]{:S(2)}) %copy-start.1) | copy-done | bytes 786456
  2.9 0.0 copy-start.2
  2.9 1.1 %copy-done.2 = bf16[128,3072]{1,0:T(8,128)(2,1)S(1)} copy-done((bf16[128,3072]{1,0:T(8,128)(2,1)S(1)}, bf16[128,3072]{1,0:T(8,128)(2,1)}, u32[]{:S(2)}) %copy-start.2) | copy-done | bytes 786456
  4.1 67.8 %shard_map.55 = bf16[128,3072]{1,0:T(8,128)(2,1)S(1)} custom-call(s32[4]{0:T(128)S(1)} %copy-done.3, bf16[128,3072]{1,0:T(8,128)(2,1)S(1)} %copy-done, bf16[128,3072]{1,0:T(8,128)(2,1)S(1)} %copy-done.1, bf16[128,3072]{1,0:T(8,128)(2,1)S(1)} %copy-done.2, s32[1,128]{1,0:T(1,128)S(1)} %bitcast.1), custom_call_target="tpu_custom_call" | custom-call | tf_op jit(solution)/shard_map/pallas_call | solution.py:415
  71.9 0.9 %copy.7 = bf16[128,3072]{1,0:T(8,128)(2,1)} copy(bf16[128,3072]{1,0:T(8,128)(2,1)S(1)} %shard_map.55) | data formatting | bytes 1572864
Async XLA Ops:
  0.0 0.7 copy-start.3
  0.0 0.7 copy-start.4
  0.7 1.1 %copy-start = (bf16[128,3072]{1,0:T(8,128)(2,1)S(1)}, bf16[128,3072]{1,0:T(8,128)(2,1)}, u32[]{:S(2)}) copy-start(bf16[128,3072]{1,0:T(8,128)(2,1)} %q_hbm.1) | copy-start | bytes 2359300
  1.8 1.1 %copy-start.1 = (bf16[128,3072]{1,0:T(8,128)(2,1)S(1)}, bf16[128,3072]{1,0:T(8,128)(2,1)}, u32[]{:S(2)}) copy-start(bf16[128,3072]{1,0:T(8,128)(2,1)} %k_hbm.1) | copy-start | bytes 2359300
  2.9 1.1 %copy-start.2 = (bf16[128,3072]{1,0:T(8,128)(2,1)S(1)}, bf16[128,3072]{1,0:T(8,128)(2,1)}, u32[]{:S(2)}) copy-start(bf16[128,3072]{1,0:T(8,128)(2,1)} %v_hbm.1) | copy-start | bytes 2359300
